TPU v7x, 32 devices: a whole 2x2x4 slice. The times are simulated.
32 devices in a mesh: groups: 2 (over x), tile: 16 (over z, y, core).
Axes of the slice: x: 2, y: 2, z: 4, core: 2. Of those that a mesh axis runs over, the one named last changes fastest.
Arguments:
- source: bfloat16 [512, 2, 69, 128], P('tile', 'groups'), parts along dimension 1, may hold values from -42 to 42
- weights: bfloat16 [1536, 128, 128], P('tile'), may hold values from -0.5 to 0.5
- block_source: int32 [1536], P('tile'), may hold values from 0 to 31
- block_target: int32 [1536], P('tile'), may hold values from 0 to 511, as said below
- edge_flip: int32 [16, 2], P('tile'), may hold values 0 or 1
- norm_gain: float32 [69], replicated, may hold values from 0.1 to 1.9
- first_kernel: bfloat16 [9, 69, 69], replicated, may hold values from -0.25 to 0.25
- second_kernel: bfloat16 [9, 69, 69], replicated, may hold values from -0.25 to 0.25
Outputs:
- gridded: bfloat16 [512, 2, 69, 128], P('tile', 'groups'), parts along dimension 1
- smoothed: bfloat16 [512, 2, 69, 128], P('tile', 'groups'), parts along dimension 1
There are 2 independent parts, one for each index of `groups`. A program takes and returns all parts, laid end to end along the dimension named above; an argument that names none is the same for every part. Nothing has to cross between parts.
Inputs may be any that keep to these rules, and one draw needn't show every extreme that they name: `block_target`: band d lies at the latitude of tile position p = d mod 2, in column d // 2. Its entries name exactly 64 distinct target rows, all in tiles c * 2 + p or c * 2 + p + 1 (any column c, positions below 2). One band names at most 8 distinct rows of one tile, and every band at position 1 names exactly 8 rows of each tile at its own position.
All inputs are finite; a program needn't handle non-finite values. No bound on the sum of `edge_flip` on one device may be relied on, other than what follows from the above.
Results may differ from a plain program's by a relative error of at most 0.001.
The roundings to bfloat16 on the way count: a program that leaves them out, or rounds other values in their place, can miss the bound.
Values may be sent and summed in bfloat16 or wider, within the bound.
No kernel may reach another device: no remote copies, remote signals or barrier semaphores. Data moves between devices by JAX's collectives and lax.ppermute only.
A program may use at most 64 MiB of HBM per device.

v0:
```python
import functools

import jax
import jax.numpy as jnp
from jax import lax
from jax.experimental import pallas as pl
from jax.experimental.pallas import tpu as pltpu
from jax.sharding import PartitionSpec as P

BLOCK = 128
CHANNELS = 69
PADDED = 72
ROWS = 32
TILE_COLS = 8
CAP = 8
GROUPS = 2 * TILE_COLS
SLOTS = GROUPS * CAP
CHUNK = 32
MARK = CHANNELS
EPSILON = 1e-05
VMEM_LIMIT = 40 * 1024 * 1024
FULL_VMEM = 60 * 1024 * 1024


def vmem():
    return pl.BlockSpec(memory_space=pltpu.VMEM)


def smem():
    return pl.BlockSpec(memory_space=pltpu.SMEM)


def split(value, size):
    if size & (size - 1) == 0:
        return value >> (size.bit_length() - 1), value & (size - 1)
    return lax.div(value, size), lax.rem(value, size)


def lanes(shape):
    return lax.broadcasted_iota(jnp.int32, shape, len(shape) - 1)


def regrid_kernel(column_rows, target_ref, index_ref, source_hbm, weight_hbm, *rest):
    same_out, next_outs = rest[0], rest[1 : 1 + TILE_COLS]
    (
        source,
        weight,
        wide,
        field,
        sums,
        rounded,
        slot_of,
        used,
        entry_slot,
        entry_fresh,
        source_sem,
        weight_sems,
        out_sems,
    ) = rest[1 + TILE_COLS :]
    entries = weight.shape[0]
    chunks = entries // CHUNK
    tile = lax.axis_index("tile")
    column, position = split(tile, column_rows)

    source_copy = pltpu.make_async_copy(source_hbm, source, source_sem)
    source_copy.start()

    def chunk_copy(chunk):
        part = pl.ds(chunk * CHUNK, CHUNK)
        return pltpu.make_async_copy(weight_hbm.at[part], weight.at[part], weight_sems.at[chunk])

    for chunk in range(chunks):
        chunk_copy(chunk).start()

    for key in range(GROUPS * ROWS):
        slot_of[key] = -1
    for group in range(GROUPS):
        used[group] = 0

    def plan(entry, carry):
        target = target_ref[entry]
        owner, row = split(target, ROWS)
        owner_column, owner_position = split(owner, column_rows)
        same = owner_position == position
        group = jnp.where(same, owner_column, TILE_COLS + (owner_column ^ column))
        key = group * ROWS + row
        known = slot_of[key]
        count = used[group]
        fresh = known < 0
        slot = jnp.where(fresh, group * CAP + count, known)
        slot_of[key] = slot
        used[group] = jnp.where(fresh, count + 1, count)
        entry_slot[entry] = slot
        entry_fresh[entry] = fresh.astype(jnp.int32)
        return carry

    lax.fori_loop(0, entries, plan, 0, unroll=4)

    tail = PADDED - 8
    for slot in range(SLOTS):
        rounded[slot, tail:] = jnp.full((8, BLOCK), ROWS, jnp.bfloat16)
    wide[pl.ds(CHANNELS * ROWS, (PADDED - CHANNELS) * ROWS), :] = jnp.zeros(
        ((PADDED - CHANNELS) * ROWS, BLOCK), jnp.float32
    )
    source_copy.wait()
    wide[pl.ds(0, CHANNELS * ROWS), :] = source[...].astype(jnp.float32)
    for row in range(ROWS):
        field[row] = wide[pl.ds(row, PADDED, stride=ROWS), :].astype(jnp.bfloat16)
    is_mark = lax.broadcasted_iota(jnp.int32, (8, BLOCK), 0) == MARK - tail

    def chunk_step(chunk, carry):
        chunk_copy(chunk).wait()
        for at in range(CHUNK):
            entry = chunk * CHUNK + at
            slot = entry_slot[entry]
            row = split(target_ref[entry], ROWS)[1]
            product = jnp.dot(
                field[index_ref[entry]], weight[entry], preferred_element_type=jnp.float32
            )
            total = jnp.where(entry_fresh[entry] == 1, 0.0, sums[slot]) + product
            sums[slot] = total
            marked = jnp.where(is_mark, row.astype(jnp.float32), total[tail:])
            rounded[slot] = jnp.concatenate([total[:tail], marked], axis=0).astype(jnp.bfloat16)
        return carry

    lax.fori_loop(0, chunks, chunk_step, 0)
    copies = [
        pltpu.make_async_copy(
            rounded.at[pl.ds(0, SLOTS // 2)], same_out, out_sems.at[0]
        )
    ]
    for group in range(TILE_COLS):
        part = rounded.at[pl.ds((TILE_COLS + group) * CAP, CAP)]
        copies.append(pltpu.make_async_copy(part, next_outs[group], out_sems.at[1 + group]))
    for copy in copies:
        copy.start()
    for copy in copies:
        copy.wait()


def regrid(target, source_index, field, weights, column_rows):
    piece = jax.ShapeDtypeStruct((CAP, PADDED, BLOCK), jnp.bfloat16)
    same = jax.ShapeDtypeStruct((TILE_COLS * CAP, PADDED, BLOCK), jnp.bfloat16)
    hbm = pl.BlockSpec(memory_space=pl.ANY)
    entries = weights.shape[0]
    return pl.pallas_call(
        functools.partial(regrid_kernel, column_rows),
        in_specs=[smem(), smem(), hbm, hbm],
        out_specs=[hbm] * (1 + TILE_COLS),
        out_shape=[same] + [piece] * TILE_COLS,
        scratch_shapes=[
            pltpu.VMEM(field.shape, jnp.bfloat16),
            pltpu.VMEM(weights.shape, jnp.bfloat16),
            pltpu.VMEM((PADDED * ROWS, BLOCK), jnp.float32),
            pltpu.VMEM((ROWS, PADDED, BLOCK), jnp.bfloat16),
            pltpu.VMEM((SLOTS, PADDED, BLOCK), jnp.float32),
            pltpu.VMEM((SLOTS, PADDED, BLOCK), jnp.bfloat16),
            pltpu.SMEM((GROUPS * ROWS,), jnp.int32),
            pltpu.SMEM((GROUPS,), jnp.int32),
            pltpu.SMEM((entries,), jnp.int32),
            pltpu.SMEM((entries,), jnp.int32),
            pltpu.SemaphoreType.DMA,
            pltpu.SemaphoreType.DMA((entries // CHUNK,)),
            pltpu.SemaphoreType.DMA((1 + TILE_COLS,)),
        ],
        compiler_params=pltpu.CompilerParams(vmem_limit_bytes=FULL_VMEM),
        name="regrid",
    )(target, source_index, field, weights)


def gather_kernel(column_rows, flip_ref, gain_ref, same, *rest):
    nexts = rest[:TILE_COLS]
    (
        gridded,
        normed,
        upward,
        downward,
        strip_out,
        summed,
        marks,
        rows,
        mark_sem,
    ) = rest[TILE_COLS:]
    position = lax.rem(lax.axis_index("tile"), column_rows)
    half = SLOTS // 2
    lane = lanes((1, BLOCK))
    mark = jnp.zeros((1, BLOCK), jnp.float32)
    for slot in range(SLOTS):
        piece = same.at[slot] if slot < half else nexts[slot // CAP - TILE_COLS].at[slot % CAP]
        mark = jnp.where(lane == slot, piece[MARK : MARK + 1].astype(jnp.float32), mark)
    marks[...] = mark.astype(jnp.int32)
    copy = pltpu.make_async_copy(marks, rows, mark_sem)
    copy.start()
    summed[...] = jnp.zeros_like(summed)
    copy.wait()

    def add(slot, piece):
        row = rows[0, slot]
        summed[row] = summed[row] + piece.astype(jnp.float32)

    def add_same(step, carry):
        for at in range(CAP):
            add(step * CAP + at, same[step * CAP + at])
        return carry

    lax.fori_loop(0, TILE_COLS, add_same, 0)

    @pl.when(position > 0)
    def _():
        for group in range(TILE_COLS):
            for place in range(CAP):
                add(half + group * CAP + place, nexts[group][place])

    gain = gain_ref[...]
    lane = lanes((PADDED, BLOCK))
    channel = lax.broadcasted_iota(jnp.int32, (PADDED, BLOCK), 0)
    strip = jnp.zeros((PADDED, BLOCK), jnp.float32)
    for row in range(ROWS):
        rounded = summed[row].astype(jnp.bfloat16)
        gridded[row] = rounded
        value = rounded.astype(jnp.float32)
        value = jnp.where(channel < CHANNELS, value, 0.0)
        square = jnp.sum(value * value, axis=0, keepdims=True) * (1.0 / CHANNELS)
        scaled = (value * lax.rsqrt(square + EPSILON) * gain).astype(jnp.bfloat16)
        normed[row] = scaled
        if row < 2:
            upward[row] = scaled
        if row >= ROWS - 2:
            downward[row - ROWS + 2] = scaled
        scaled = scaled.astype(jnp.float32)
        for place, column in enumerate(STRIP_COLUMNS):
            at = place * ROWS + row
            strip = jnp.where(lane == at, pltpu.roll(scaled, (at - column) % BLOCK, 1), strip)
    for side in range(2):
        strip = jnp.where(channel == CHANNELS + side, flip_ref[0, side].astype(jnp.float32), strip)
    strip = strip.astype(jnp.bfloat16)
    upward[2] = strip
    downward[2] = strip
    strip_out[...] = strip


FIELD = jax.ShapeDtypeStruct((ROWS, PADDED, BLOCK), jnp.bfloat16)
RIM = jax.ShapeDtypeStruct((3, PADDED, BLOCK), jnp.bfloat16)
STRIP_COLUMNS = (0, 1, BLOCK - 2, BLOCK - 1)
STRIP = jax.ShapeDtypeStruct((PADDED, BLOCK), jnp.bfloat16)


def gather_rows(column_rows, edge_flip, gain, same, nexts):
    return pl.pallas_call(
        functools.partial(gather_kernel, column_rows),
        in_specs=[smem()] + [vmem()] * (2 + TILE_COLS),
        out_specs=[vmem()] * 5,
        out_shape=[FIELD, FIELD, RIM, RIM, STRIP],
        scratch_shapes=[
            pltpu.VMEM((ROWS + 1, PADDED, BLOCK), jnp.float32),
            pltpu.VMEM((1, SLOTS), jnp.int32),
            pltpu.SMEM((1, SLOTS), jnp.int32),
            pltpu.SemaphoreType.DMA,
        ],
        compiler_params=pltpu.CompilerParams(vmem_limit_bytes=VMEM_LIMIT),
        name="gather_rows",
    )(edge_flip, gain, same, *nexts)


def turn_kernel(field, out, turned):
    for row in range(ROWS):
        turned[pl.ds(row, PADDED, stride=ROWS), :] = field[row].astype(jnp.float32)
    out[...] = turned[pl.ds(0, CHANNELS * ROWS), :].astype(jnp.bfloat16)


def channels_first(field):
    return pl.pallas_call(
        turn_kernel,
        in_specs=[vmem()],
        out_specs=vmem(),
        out_shape=jax.ShapeDtypeStruct((CHANNELS * ROWS, BLOCK), jnp.bfloat16),
        scratch_shapes=[pltpu.VMEM((PADDED * ROWS, BLOCK), jnp.float32)],
        compiler_params=pltpu.CompilerParams(vmem_limit_bytes=VMEM_LIMIT),
        name="channels_first",
    )(field)


def strip_plan(column_rows):
    if column_rows == 2:
        return [], 3, 1
    return [-2, 2], column_rows, 2


def conv_kernel(
    column_rows, first_taps_ref, second_taps_ref, field, gridded, above, below, own_strip, *rest
):
    near, far, reach = strip_plan(column_rows)
    near_strips, (west_pack, east_pack) = rest[: len(near)], rest[len(near) : len(near) + 2]
    smoothed, hidden, partial, turned = rest[len(near) + 2 :]
    count = lax.axis_size("tile")
    tile = lax.axis_index("tile")
    lane = lanes((PADDED, BLOCK))
    last = ROWS + 1
    R = column_rows

    strips = {-1: above[2], 0: own_strip[...], 1: below[2]}
    strips.update((shift, ref[...]) for shift, ref in zip(near, near_strips))
    for at in range(-reach, reach + 1):
        strips[at - far], strips[at + far] = west_pack[at + reach], east_pack[at + reach]
    strips = {shift: value.astype(jnp.float32) for shift, value in strips.items()}

    def place(shift):
        return lax.rem(tile + shift + count, count)

    def ends(shift, before, after, middle):
        before = jnp.where(place(shift) > 0, before, 0.0)
        after = jnp.where(place(shift) < count - 1, after, 0.0)
        return jnp.where(lane == 0, before, jnp.where(lane == last, after, middle))

    memo = {}

    def padded_column(shift, which):
        if (shift, which) not in memo:
            base = which * ROWS
            memo[shift, which] = ends(
                shift,
                pltpu.roll(strips[shift - 1], (1 - base - ROWS) % BLOCK, 1),
                pltpu.roll(strips[shift + 1], (last - base) % BLOCK, 1),
                pltpu.roll(strips[shift], (1 - base) % BLOCK, 1),
            )
        return memo[shift, which]

    row_id = lax.broadcasted_iota(jnp.int32, (BLOCK, BLOCK), 0)
    reversal = (row_id + lanes((BLOCK, BLOCK)) == last).astype(jnp.bfloat16)

    def reversed_lanes(planes):
        stacked = jnp.concatenate(planes, axis=0).astype(jnp.bfloat16)
        turned_round = jnp.dot(stacked, reversal, preferred_element_type=jnp.float32)
        return [turned_round[at * PADDED : (at + 1) * PADDED] for at in range(len(planes))]

    west_of = {shift: (shift - R, 3) for shift in {-1, 0, 1, R - 1, R, R + 1}}
    east_of = {shift: (shift + R, 0) for shift in {-1, 0, 1, -R - 1, -R, -R + 1}}
    keys = sorted(set(west_of.values()) | set(east_of.values()))
    flipped = dict(zip(keys, reversed_lanes([padded_column(*key) for key in keys])))

    def side(shift, which, table):
        key = table[shift]
        flip = strips[shift][CHANNELS + which : CHANNELS + which + 1] > 0.5
        return jnp.where(flip, flipped[key], padded_column(*key))

    west = {shift: side(shift, 0, west_of) for shift in sorted(west_of)}
    east = {shift: side(shift, 1, east_of) for shift in sorted(east_of)}

    def columns(value, west_plane, west_row, east_plane, east_row):
        value = value.astype(jnp.float32)
        west_value = pltpu.roll(west_plane, (BLOCK - west_row) % BLOCK, 1)
        east_value = pltpu.roll(east_plane, BLOCK - 1 - east_row, 1)
        left = jnp.where(lane == 0, west_value, pltpu.roll(value, 1, 1))
        right = jnp.where(lane == BLOCK - 1, east_value, pltpu.roll(value, BLOCK - 1, 1))
        return jnp.concatenate([left, value, right], axis=0).astype(jnp.bfloat16)

    def tap_sums(taps, one, two):
        both = jnp.concatenate([one, two], axis=1)
        result = jnp.dot(taps, both, preferred_element_type=jnp.float32)
        return result[:, :BLOCK], result[:, BLOCK:]

    def all_rows(taps, read, west_plane, east_plane):
        for p in range(0, ROWS + 2, 2):
            partial[p], partial[p + 1] = tap_sums(
                taps,
                columns(read(p), west_plane, p, east_plane, p),
                columns(read(p + 1), west_plane, p + 1, east_plane, p + 1),
            )

    def conv_row(row):
        return (
            partial[row, :PADDED]
            + partial[row + 1, PADDED : 2 * PADDED]
            + partial[row + 2, 2 * PADDED :]
        )

    def activated(value):
        return jax.nn.gelu(value).astype(jnp.bfloat16)

    first_taps = first_taps_ref[...]
    up = [jnp.where(tile > 0, above[at], 0.0) for at in range(2)]
    down = [jnp.where(tile < count - 1, below[at], 0.0) for at in range(2)]

    def read_normed(p):
        return up[1] if p == 0 else down[0] if p == last else field[p - 1]

    all_rows(first_taps, read_normed, west[0], east[0])
    for row in range(ROWS):
        hidden[row + 1] = activated(conv_row(row))

    upper, lower = 0.0, 0.0
    for at, (high, low) in enumerate(
        [(up[0], field[ROWS - 1]), (up[1], down[0]), (field[0], down[1])]
    ):
        from_row = ROWS - 1 + at
        one, two = tap_sums(
            first_taps,
            columns(high, west[-1], from_row, east[-1], from_row),
            columns(low, west[1], at, east[1], at),
        )
        upper += one[at * PADDED : (at + 1) * PADDED]
        lower += two[at * PADDED : (at + 1) * PADDED]
    hidden[0] = jnp.where(tile > 0, activated(upper), 0.0)
    hidden[last] = jnp.where(tile < count - 1, activated(lower), 0.0)

    def along(result):
        raw = (
            result[:PADDED]
            + pltpu.roll(result[PADDED : 2 * PADDED], BLOCK - 1, 1)
            + pltpu.roll(result[2 * PADDED :], BLOCK - 2, 1)
        )
        return activated(raw).astype(jnp.float32)

    west_hidden, east_hidden = {}, {}
    for at in (-1, 0, 1):
        q = at - R
        one = [padded_column(q, 2), padded_column(q, 3), east[q]]
        q = at + R
        two = [west[q], padded_column(q, 0), padded_column(q, 1)]
        one, two = tap_sums(
            first_taps,
            jnp.concatenate(one, axis=0).astype(jnp.bfloat16),
            jnp.concatenate(two, axis=0).astype(jnp.bfloat16),
        )
        west_hidden[at], east_hidden[at] = along(one), along(two)

    def hidden_side(shift, values):
        return ends(
            shift,
            pltpu.roll(values[-1], BLOCK - ROWS + 1, 1),
            pltpu.roll(values[1], last, 1),
            pltpu.roll(values[0], 1, 1),
        )

    sides = [hidden_side(-R, west_hidden), hidden_side(R, east_hidden)]
    for which, turned_side in enumerate(reversed_lanes(sides)):
        flip = strips[0][CHANNELS + which : CHANNELS + which + 1] > 0.5
        sides[which] = jnp.where(flip, turned_side, sides[which])

    all_rows(second_taps_ref[...], lambda p: hidden[p], sides[0], sides[1])
    for row in range(ROWS):
        turned[pl.ds(row, PADDED, stride=ROWS), :] = gridded[row].astype(jnp.float32) + conv_row(row)
    smoothed[...] = turned[pl.ds(0, CHANNELS * ROWS), :].astype(jnp.bfloat16)


def convolutions(column_rows, first_taps, second_taps, field, gridded, rims, own_strip, strips):
    operands = [first_taps, second_taps, field, gridded, *rims, own_strip, *strips]
    return pl.pallas_call(
        functools.partial(conv_kernel, column_rows),
        in_specs=[vmem()] * len(operands),
        out_specs=vmem(),
        out_shape=jax.ShapeDtypeStruct((CHANNELS * ROWS, BLOCK), jnp.bfloat16),
        scratch_shapes=[
            pltpu.VMEM((ROWS + 2, PADDED, BLOCK), jnp.bfloat16),
            pltpu.VMEM((ROWS + 2, 3 * PADDED, BLOCK), jnp.float32),
            pltpu.VMEM((PADDED * ROWS, BLOCK), jnp.float32),
        ],
        compiler_params=pltpu.CompilerParams(vmem_limit_bytes=VMEM_LIMIT),
        name="convolutions",
    )(*operands)


def tap_matrix(kernel):
    pad = PADDED - CHANNELS
    taps = jnp.pad(kernel, ((0, 0), (0, pad), (0, pad))).reshape(3, 3, PADDED, PADDED)
    return taps.transpose(0, 2, 1, 3).reshape(3 * PADDED, 3 * PADDED)


def from_shift(value, shift):
    count = lax.axis_size("tile")
    return lax.ppermute(value, "tile", [(i, (i - shift) % count) for i in range(count)])


def per_device(
    source, weights, block_source, block_target, edge_flip, norm_gain, first_kernel, second_kernel
):
    count = lax.axis_size("tile")
    column_rows = count // TILE_COLS
    field = source.reshape(ROWS, CHANNELS, BLOCK).transpose(1, 0, 2).reshape(-1, BLOCK)
    same, *nexts = regrid(block_target, block_source, field, weights, column_rows)

    for across in (0, 7, 3, 6, 2, 5, 1, 4):
        pairs = [
            (c * column_rows + p, (c ^ across) * column_rows + p + 1)
            for c in range(TILE_COLS)
            for p in range(column_rows - 1)
        ]
        nexts[across] = lax.ppermute(nexts[across], "tile", pairs)
    same = lax.all_to_all(
        same,
        "tile",
        0,
        0,
        axis_index_groups=[
            [c * column_rows + p for c in range(TILE_COLS)] for p in range(column_rows)
        ],
        tiled=True,
    )

    gain = jnp.broadcast_to(
        jnp.pad(norm_gain, (0, PADDED - CHANNELS))[:, None], (PADDED, BLOCK)
    )
    first_taps, second_taps = tap_matrix(first_kernel), tap_matrix(second_kernel)
    same, nexts, gain, first_taps, second_taps = lax.optimization_barrier(
        (same, nexts, gain, first_taps, second_taps)
    )
    gridded, normed, upward, downward, strip = gather_rows(
        column_rows, edge_flip, gain, same, nexts
    )
    rims = [from_shift(downward, -1), from_shift(upward, 1)]
    near, far, reach = strip_plan(column_rows)
    strips = [from_shift(strip, shift) for shift in near]
    held = {-1: rims[0][2], 0: strip, 1: rims[1][2], **dict(zip(near, strips))}
    pack = jnp.stack([held[at] for at in range(-reach, reach + 1)])
    strips += [from_shift(pack, -far), from_shift(pack, far)]
    gridded_out = channels_first(gridded)
    smoothed = convolutions(
        column_rows, first_taps, second_taps, normed, gridded, rims, strip, strips
    )

    def placed(value):
        return value.reshape(CHANNELS, ROWS, BLOCK).transpose(1, 0, 2)[:, None]

    return placed(gridded_out), placed(smoothed)


def solution(mesh):
    in_specs = (
        P("tile", "groups", None, None),
        P("tile", None, None),
        P("tile"),
        P("tile"),
        P("tile", None),
        P(),
        P(),
        P(),
    )
    out_specs = (P("tile", "groups", None, None), P("tile", "groups", None, None))
    return jax.shard_map(
        per_device, mesh=mesh, in_specs=in_specs, out_specs=out_specs, check_vma=False
    )
```

profile of v0, /device:TPU:1, one launch (start us, length us, event | category | flops | bytes accessed | tf_op | source)
XLA Modules:
  0.0 72.3 jit_solution(748126479839502204)
XLA Ops:
  0.6 6.2 %regrid.1 = (bf16[64,72,128]{2,1,0:T(8,128)(2,1)}, bf16[8,72,128]{2,1,0:T(8,128)(2,1)}, bf16[8,72,128]{2,1,0:T(8,128)(2,1)}, bf16[8,72,128]{2,1,0:T(8,128)(2,1)}...) custom-call(s32[96]{0:T(128)} %target_ref.1, ...), custom_call_target="tpu_custom_call" | custom-call | tf_op jit(solution)/shard_map/regrid/pallas_call | solution.py:146
  6.8 0.0 copy-start.8
  6.8 0.0 copy-start.7
  6.8 0.0 copy-start.6
  6.8 0.0 copy-start.5
  6.8 0.0 copy-start.4
  6.8 0.0 copy-start.3
  6.9 0.0 copy-start.1
  6.9 0.0 copy-start.2
  6.9 6.5 %all-to-all-start = ((bf16[64,72,128]{2,1,0:T(8,128)(2,1)}), bf16[64,72,128]{2,1,0:T(8,128)(2,1)S(1)}, u32[]{:S(2)}, u32[]{:S(2)}) async-start(bf16[64,72,128]{2,1,0:T(8,128)(2,1)} %get-tuple-element.28), calls=%async_computation | async-start | bytes 2359296 | tf_op jit(solution)/shard_map/all_to_all | solution.py:489
  13.4 0.0 copy-start
  13.4 0.0 copy-done.8
  13.4 1.3 %collective-permute-start = (bf16[8,72,128]{2,1,0:T(8,128)(2,1)S(1)}, bf16[8,72,128]{2,1,0:T(8,128)(2,1)S(1)}, u32[]{:S(2)}, u32[]{:S(2)}) collective-permute-start(bf16[8,72,128]{2,1,0:T(8,128)(2,1)S(1)} %copy-done.8), channel_id=1, source_target_pairs={{0,1},{2,3},{4,5},{6,7},{8,9},{10,11},{12,13},{14,15},{16,17},{18,... | collective-permute-start | bytes 442376 | tf_op jit(solution)/shard_map/ppermute | solution.py:488
  14.7 1.3 %collective-permute-start.1 = (bf16[8,72,128]{2,1,0:T(8,128)(2,1)S(1)}, bf16[8,72,128]{2,1,0:T(8,128)(2,1)S(1)}, u32[]{:S(2)}, u32[]{:S(2)}) collective-permute-start(bf16[8,72,128]{2,1,0:T(8,128)(2,1)S(1)} %copy-done.7), channel_id=1, source_target_pairs={{0,3},{2,1},{4,7},{6,5},{8,11},{10,9},{12,15},{14,13},{16,19},{18,... | collective-permute-start | bytes 442376 | tf_op jit(solution)/shard_map/ppermute | solution.py:488
  16.0 1.3 %collective-permute-start.2 = (bf16[8,72,128]{2,1,0:T(8,128)(2,1)S(1)}, bf16[8,72,128]{2,1,0:T(8,128)(2,1)S(1)}, u32[]{:S(2)}, u32[]{:S(2)}) collective-permute-start(bf16[8,72,128]{2,1,0:T(8,128)(2,1)S(1)} %copy-done.6), channel_id=1, source_target_pairs={{0,5},{2,7},{4,1},{6,3},{8,13},{10,15},{12,9},{14,11},{16,21},{18,... | collective-permute-start | bytes 442376 | tf_op jit(solution)/shard_map/ppermute | solution.py:488
  17.3 1.3 %collective-permute-start.3 = (bf16[8,72,128]{2,1,0:T(8,128)(2,1)}, bf16[8,72,128]{2,1,0:T(8,128)(2,1)S(1)}, u32[]{:S(2)}, u32[]{:S(2)}) collective-permute-start(bf16[8,72,128]{2,1,0:T(8,128)(2,1)} %get-tuple-element.32), channel_id=1, source_target_pairs={{0,7},{2,5},{4,3},{6,1},{8,15},{10,13},{12,11},{14,9},{16,23},{18,... | collective-permute-start | bytes 442376 | tf_op jit(solution)/shard_map/ppermute | solution.py:488
  18.6 1.3 %collective-permute-start.4 = (bf16[8,72,128]{2,1,0:T(8,128)(2,1)}, bf16[8,72,128]{2,1,0:T(8,128)(2,1)S(1)}, u32[]{:S(2)}, u32[]{:S(2)}) collective-permute-start(bf16[8,72,128]{2,1,0:T(8,128)(2,1)} %get-tuple-element.33), channel_id=1, source_target_pairs={{0,9},{2,11},{4,13},{6,15},{8,1},{10,3},{12,5},{14,7},{16,25},{18,... | collective-permute-start | bytes 442376 | tf_op jit(solution)/shard_map/ppermute | solution.py:488
  19.9 0.0 collective-permute-done.rest_0_
  20.0 1.3 %collective-permute-start.5 = (bf16[8,72,128]{2,1,0:T(8,128)(2,1)S(1)}, bf16[8,72,128]{2,1,0:T(8,128)(2,1)S(1)}, u32[]{:S(2)}, u32[]{:S(2)}) collective-permute-start(bf16[8,72,128]{2,1,0:T(8,128)(2,1)S(1)} %copy-done.5), channel_id=1, source_target_pairs={{0,11},{2,9},{4,15},{6,13},{8,3},{10,1},{12,7},{14,5},{16,27},{18,... | collective-permute-start | bytes 442376 | tf_op jit(solution)/shard_map/ppermute | solution.py:488
  21.3 4.0 %collective-permute-done.1.rest_1_ = bf16[8,72,128]{2,1,0:T(8,128)(2,1)S(1)} collective-permute-done((bf16[8,72,128]{2,1,0:T(8,128)(2,1)S(1)}, bf16[8,72,128]{2,1,0:T(8,128)(2,1)S(1)}, u32[]{:S(2)}, u32[]{:S(2)}) %collective-permute-start.1) | collective-permute-done | bytes 147488 | tf_op jit(solution)/shard_map/ppermute | solution.py:488
  25.3 1.3 %collective-permute-start.6 = (bf16[8,72,128]{2,1,0:T(8,128)(2,1)S(1)}, bf16[8,72,128]{2,1,0:T(8,128)(2,1)S(1)}, u32[]{:S(2)}, u32[]{:S(2)}) collective-permute-start(bf16[8,72,128]{2,1,0:T(8,128)(2,1)S(1)} %copy-done.4), channel_id=1, source_target_pairs={{0,13},{2,15},{4,9},{6,11},{8,5},{10,7},{12,1},{14,3},{16,29},{18,... | collective-permute-start | bytes 442376 | tf_op jit(solution)/shard_map/ppermute | solution.py:488
  26.6 4.7 %collective-permute-done.2.rest_2_ = bf16[8,72,128]{2,1,0:T(8,128)(2,1)S(1)} collective-permute-done((bf16[8,72,128]{2,1,0:T(8,128)(2,1)S(1)}, bf16[8,72,128]{2,1,0:T(8,128)(2,1)S(1)}, u32[]{:S(2)}, u32[]{:S(2)}) %collective-permute-start.2) | collective-permute-done | bytes 147488 | tf_op jit(solution)/shard_map/ppermute | solution.py:488
  31.3 0.0 copy-done.3
  31.3 1.3 %collective-permute-start.7 = (bf16[8,72,128]{2,1,0:T(8,128)(2,1)S(1)}, bf16[8,72,128]{2,1,0:T(8,128)(2,1)S(1)}, u32[]{:S(2)}, u32[]{:S(2)}) collective-permute-start(bf16[8,72,128]{2,1,0:T(8,128)(2,1)S(1)} %copy-done.3), channel_id=1, source_target_pairs={{0,15},{2,13},{4,11},{6,9},{8,7},{10,5},{12,3},{14,1},{16,31},{18,... | collective-permute-start | bytes 442376 | tf_op jit(solution)/shard_map/ppermute | solution.py:488
  32.6 0.0 copy-done.1
  32.6 0.1 copy.17
  32.7 0.1 reshape.32.first_taps_ref
  32.9 0.0 copy-done.2
  32.9 0.1 copy.16
  33.0 0.1 reshape.34.second_taps_ref
  33.2 2.9 %collective-permute-done.3.rest_3_ = bf16[8,72,128]{2,1,0:T(8,128)(2,1)S(1)} collective-permute-done((bf16[8,72,128]{2,1,0:T(8,128)(2,1)}, bf16[8,72,128]{2,1,0:T(8,128)(2,1)S(1)}, u32[]{:S(2)}, u32[]{:S(2)}) %collective-permute-start.3) | collective-permute-done | bytes 147488 | tf_op jit(solution)/shard_map/ppermute | solution.py:488
  36.1 14.1 %collective-permute-done.4.rest_4_ = bf16[8,72,128]{2,1,0:T(8,128)(2,1)S(1)} collective-permute-done((bf16[8,72,128]{2,1,0:T(8,128)(2,1)}, bf16[8,72,128]{2,1,0:T(8,128)(2,1)S(1)}, u32[]{:S(2)}, u32[]{:S(2)}) %collective-permute-start.4) | collective-permute-done | bytes 147488 | tf_op jit(solution)/shard_map/ppermute | solution.py:488
  50.1 2.5 %collective-permute-done.5.rest_5_ = bf16[8,72,128]{2,1,0:T(8,128)(2,1)S(1)} collective-permute-done((bf16[8,72,128]{2,1,0:T(8,128)(2,1)S(1)}, bf16[8,72,128]{2,1,0:T(8,128)(2,1)S(1)}, u32[]{:S(2)}, u32[]{:S(2)}) %collective-permute-start.5) | collective-permute-done | bytes 147488 | tf_op jit(solution)/shard_map/ppermute | solution.py:488
  52.7 0.0 collective-permute-done.6.rest_6_
  52.7 0.0 collective-permute-done.7.rest_7_
  52.7 0.0 all-to-all-done.same
  52.7 0.1 broadcast_in_dim.12.gain_ref
  52.8 2.8 %gather_rows.1 = (bf16[32,72,128]{2,1,0:T(8,128)(2,1)S(1)}, bf16[32,72,128]{2,1,0:T(8,128)(2,1)S(1)}, bf16[3,72,128]{2,1,0:T(8,128)(2,1)S(1)}, bf16[3,72,128]{2,1,0:T(8,128)(2,1)S(1)}, bf16[72,128]{1,0:T(8,128)(2,1)S(1)}) custom-call(s32[1,2]{1,0:T(1,128)S(1)} %copy-done, f32[72,128]{1,0:T(8,128)S(1)} %broadcast_in_dim.12.gain_ref, ...), custom_call_target="tpu_custom_call" | custom-call | tf_op jit(solution)/shard_map/gather_rows/pallas_call | solution.py:249
  55.5 0.1 collective-permute-start.8
  55.6 0.5 collective-permute-start.9
  56.1 0.7 %collective-permute-done.8.above = bf16[3,72,128]{2,1,0:T(8,128)(2,1)S(1)} collective-permute-done((bf16[3,72,128]{2,1,0:T(8,128)(2,1)S(1)}, bf16[3,72,128]{2,1,0:T(8,128)(2,1)S(1)}, u32[]{:S(2)}, u32[]{:S(2)}) %collective-permute-start.8) | collective-permute-done | bytes 55328 | tf_op jit(solution)/shard_map/ppermute | solution.py:471
  56.8 2.4 %collective-permute-done.9.below = bf16[3,72,128]{2,1,0:T(8,128)(2,1)S(1)} collective-permute-done((bf16[3,72,128]{2,1,0:T(8,128)(2,1)S(1)}, bf16[3,72,128]{2,1,0:T(8,128)(2,1)S(1)}, u32[]{:S(2)}, u32[]{:S(2)}) %collective-permute-start.9) | collective-permute-done | bytes 55328 | tf_op jit(solution)/shard_map/ppermute | solution.py:471
  59.2 0.9 %collective-permute-start.11 = (bf16[3,72,128]{2,1,0:T(8,128)(2,1)S(1)}, bf16[3,72,128]{2,1,0:T(8,128)(2,1)S(1)}, u32[]{:S(2)}, u32[]{:S(2)}) collective-permute-start(bf16[3,72,128]{2,1,0:T(8,128)(2,1)S(1)} %pad_maximum_fusion), channel_id=1, source_target_pairs={{0,13},{1,14},{2,15},{3,0},{4,1},{5,2},{6,3},{7,4},{8,5},{9,6},{10... | collective-permute-start | bytes 165896 | tf_op jit(solution)/shard_map/ppermute | solution.py:471
  60.1 1.2 %collective-permute-start.10 = (bf16[3,72,128]{2,1,0:T(8,128)(2,1)S(1)}, bf16[3,72,128]{2,1,0:T(8,128)(2,1)S(1)}, u32[]{:S(2)}, u32[]{:S(2)}) collective-permute-start(bf16[3,72,128]{2,1,0:T(8,128)(2,1)S(1)} %pad_maximum_fusion), channel_id=1, source_target_pairs={{0,3},{1,4},{2,5},{3,6},{4,7},{5,8},{6,9},{7,10},{8,11},{9,12},{10... | collective-permute-start | bytes 165896 | tf_op jit(solution)/shard_map/ppermute | solution.py:471
  61.3 2.0 %channels_first.1 = bf16[2208,128]{1,0:T(8,128)(2,1)} custom-call(bf16[32,72,128]{2,1,0:T(8,128)(2,1)S(1)} %get-tuple-element.47.field.gridded), custom_call_target="tpu_custom_call" | custom-call | tf_op jit(solution)/shard_map/channels_first/pallas_call | solution.py:272
  63.3 0.0 collective-permute-done.11.rest_1_
  63.3 4.1 %collective-permute-done.10.rest_0_ = bf16[3,72,128]{2,1,0:T(8,128)(2,1)S(1)} collective-permute-done((bf16[3,72,128]{2,1,0:T(8,128)(2,1)S(1)}, bf16[3,72,128]{2,1,0:T(8,128)(2,1)S(1)}, u32[]{:S(2)}, u32[]{:S(2)}) %collective-permute-start.10) | collective-permute-done | bytes 55328 | tf_op jit(solution)/shard_map/ppermute | solution.py:471
  67.5 4.8 %convolutions.1 = bf16[2208,128]{1,0:T(8,128)(2,1)} custom-call(bf16[216,216]{1,0:T(8,128)(2,1)S(1)} %reshape.32.first_taps_ref, bf16[216,216]{1,0:T(8,128)(2,1)S(1)} %reshape.34.second_taps_ref, bf16[32,72,128]{2,1,0:T(8,128)(2,1)S(1)} %get-tuple-element.50.field, bf16[32,72,128]{2,1,0:T(8,128)(2,1)S(1)} %get-tuple-element.47.field.gridded, ...), custom_call_target="tpu_custom_call" | custom-call | tf_op jit(solution)/shard_map/convolutions/pallas_call | solution.py:448
  (13 shorter events, 0.1 us)
Async XLA Ops:
  6.8 6.6 %copy-start.8 = (bf16[8,72,128]{2,1,0:T(8,128)(2,1)S(1)}, bf16[8,72,128]{2,1,0:T(8,128)(2,1)}, u32[]{:S(2)}) copy-start(bf16[8,72,128]{2,1,0:T(8,128)(2,1)} %get-tuple-element.29) | copy-start | bytes 442372
  6.8 7.9 %copy-start.7 = (bf16[8,72,128]{2,1,0:T(8,128)(2,1)S(1)}, bf16[8,72,128]{2,1,0:T(8,128)(2,1)}, u32[]{:S(2)}) copy-start(bf16[8,72,128]{2,1,0:T(8,128)(2,1)} %get-tuple-element.30) | copy-start | bytes 442372
  6.8 9.2 %copy-start.6 = (bf16[8,72,128]{2,1,0:T(8,128)(2,1)S(1)}, bf16[8,72,128]{2,1,0:T(8,128)(2,1)}, u32[]{:S(2)}) copy-start(bf16[8,72,128]{2,1,0:T(8,128)(2,1)} %get-tuple-element.31) | copy-start | bytes 442372
  6.8 13.1 %copy-start.5 = (bf16[8,72,128]{2,1,0:T(8,128)(2,1)S(1)}, bf16[8,72,128]{2,1,0:T(8,128)(2,1)}, u32[]{:S(2)}) copy-start(bf16[8,72,128]{2,1,0:T(8,128)(2,1)} %get-tuple-element.34) | copy-start | bytes 442372
  6.8 18.5 %copy-start.4 = (bf16[8,72,128]{2,1,0:T(8,128)(2,1)S(1)}, bf16[8,72,128]{2,1,0:T(8,128)(2,1)}, u32[]{:S(2)}) copy-start(bf16[8,72,128]{2,1,0:T(8,128)(2,1)} %get-tuple-element.35) | copy-start | bytes 442372
  6.8 24.4 %copy-start.3 = (bf16[8,72,128]{2,1,0:T(8,128)(2,1)S(1)}, bf16[8,72,128]{2,1,0:T(8,128)(2,1)}, u32[]{:S(2)}) copy-start(bf16[8,72,128]{2,1,0:T(8,128)(2,1)} %get-tuple-element.36) | copy-start | bytes 442372
  6.9 25.7 %copy-start.1 = (bf16[9,69,69]{2,1,0:T(8,128)(2,1)S(1)}, bf16[9,69,69]{2,1,0:T(8,128)(2,1)}, u32[]{:S(2)}) copy-start(bf16[9,69,69]{2,1,0:T(8,128)(2,1)} %param.14) | copy-start | bytes 257098
  6.9 26.0 %copy-start.2 = (bf16[9,69,69]{2,1,0:T(8,128)(2,1)S(1)}, bf16[9,69,69]{2,1,0:T(8,128)(2,1)}, u32[]{:S(2)}) copy-start(bf16[9,69,69]{2,1,0:T(8,128)(2,1)} %param.15) | copy-start | bytes 257098
  6.9 45.8 %all-to-all-start = ((bf16[64,72,128]{2,1,0:T(8,128)(2,1)}), bf16[64,72,128]{2,1,0:T(8,128)(2,1)S(1)}, u32[]{:S(2)}, u32[]{:S(2)}) async-start(bf16[64,72,128]{2,1,0:T(8,128)(2,1)} %get-tuple-element.28), calls=%async_computation | async-start | bytes 2359296 | tf_op jit(solution)/shard_map/all_to_all | solution.py:489
  13.4 19.8 %copy-start.9 = (f32[69]{0:T(128)S(1)}, f32[69]{0:T(128)}, u32[]{:S(2)}) copy-start(f32[69]{0:T(128)} %param.13) | copy-start | bytes 832
  13.4 39.3 %copy-start = (s32[1,2]{1,0:T(1,128)S(1)}, s32[1,2]{1,0:T(1,128)}, u32[]{:S(2)}) copy-start(s32[1,2]{1,0:T(1,128)} %flip_ref.1) | copy-start | bytes 28
  13.4 6.5 %collective-permute-start = (bf16[8,72,128]{2,1,0:T(8,128)(2,1)S(1)}, bf16[8,72,128]{2,1,0:T(8,128)(2,1)S(1)}, u32[]{:S(2)}, u32[]{:S(2)}) collective-permute-start(bf16[8,72,128]{2,1,0:T(8,128)(2,1)S(1)} %copy-done.8), channel_id=1, source_target_pairs={{0,1},{2,3},{4,5},{6,7},{8,9},{10,11},{12,13},{14,15},{16,17},{18,... | collective-permute-start | bytes 442376 | tf_op jit(solution)/shard_map/ppermute | solution.py:488
  14.7 10.6 %collective-permute-start.1 = (bf16[8,72,128]{2,1,0:T(8,128)(2,1)S(1)}, bf16[8,72,128]{2,1,0:T(8,128)(2,1)S(1)}, u32[]{:S(2)}, u32[]{:S(2)}) collective-permute-start(bf16[8,72,128]{2,1,0:T(8,128)(2,1)S(1)} %copy-done.7), channel_id=1, source_target_pairs={{0,3},{2,1},{4,7},{6,5},{8,11},{10,9},{12,15},{14,13},{16,19},{18,... | collective-permute-start | bytes 442376 | tf_op jit(solution)/shard_map/ppermute | solution.py:488
  16.0 15.2 %collective-permute-start.2 = (bf16[8,72,128]{2,1,0:T(8,128)(2,1)S(1)}, bf16[8,72,128]{2,1,0:T(8,128)(2,1)S(1)}, u32[]{:S(2)}, u32[]{:S(2)}) collective-permute-start(bf16[8,72,128]{2,1,0:T(8,128)(2,1)S(1)} %copy-done.6), channel_id=1, source_target_pairs={{0,5},{2,7},{4,1},{6,3},{8,13},{10,15},{12,9},{14,11},{16,21},{18,... | collective-permute-start | bytes 442376 | tf_op jit(solution)/shard_map/ppermute | solution.py:488
  17.3 18.7 %collective-permute-start.3 = (bf16[8,72,128]{2,1,0:T(8,128)(2,1)}, bf16[8,72,128]{2,1,0:T(8,128)(2,1)S(1)}, u32[]{:S(2)}, u32[]{:S(2)}) collective-permute-start(bf16[8,72,128]{2,1,0:T(8,128)(2,1)} %get-tuple-element.32), channel_id=1, source_target_pairs={{0,7},{2,5},{4,3},{6,1},{8,15},{10,13},{12,11},{14,9},{16,23},{18,... | collective-permute-start | bytes 442376 | tf_op jit(solution)/shard_map/ppermute | solution.py:488
  18.6 31.5 %collective-permute-start.4 = (bf16[8,72,128]{2,1,0:T(8,128)(2,1)}, bf16[8,72,128]{2,1,0:T(8,128)(2,1)S(1)}, u32[]{:S(2)}, u32[]{:S(2)}) collective-permute-start(bf16[8,72,128]{2,1,0:T(8,128)(2,1)} %get-tuple-element.33), channel_id=1, source_target_pairs={{0,9},{2,11},{4,13},{6,15},{8,1},{10,3},{12,5},{14,7},{16,25},{18,... | collective-permute-start | bytes 442376 | tf_op jit(solution)/shard_map/ppermute | solution.py:488
  20.0 32.7 %collective-permute-start.5 = (bf16[8,72,128]{2,1,0:T(8,128)(2,1)S(1)}, bf16[8,72,128]{2,1,0:T(8,128)(2,1)S(1)}, u32[]{:S(2)}, u32[]{:S(2)}) collective-permute-start(bf16[8,72,128]{2,1,0:T(8,128)(2,1)S(1)} %copy-done.5), channel_id=1, source_target_pairs={{0,11},{2,9},{4,15},{6,13},{8,3},{10,1},{12,7},{14,5},{16,27},{18,... | collective-permute-start | bytes 442376 | tf_op jit(solution)/shard_map/ppermute | solution.py:488
  25.3 27.4 %collective-permute-start.6 = (bf16[8,72,128]{2,1,0:T(8,128)(2,1)S(1)}, bf16[8,72,128]{2,1,0:T(8,128)(2,1)S(1)}, u32[]{:S(2)}, u32[]{:S(2)}) collective-permute-start(bf16[8,72,128]{2,1,0:T(8,128)(2,1)S(1)} %copy-done.4), channel_id=1, source_target_pairs={{0,13},{2,15},{4,9},{6,11},{8,5},{10,7},{12,1},{14,3},{16,29},{18,... | collective-permute-start | bytes 442376 | tf_op jit(solution)/shard_map/ppermute | solution.py:488
  31.3 21.4 %collective-permute-start.7 = (bf16[8,72,128]{2,1,0:T(8,128)(2,1)S(1)}, bf16[8,72,128]{2,1,0:T(8,128)(2,1)S(1)}, u32[]{:S(2)}, u32[]{:S(2)}) collective-permute-start(bf16[8,72,128]{2,1,0:T(8,128)(2,1)S(1)} %copy-done.3), channel_id=1, source_target_pairs={{0,15},{2,13},{4,11},{6,9},{8,7},{10,5},{12,3},{14,1},{16,31},{18,... | collective-permute-start | bytes 442376 | tf_op jit(solution)/shard_map/ppermute | solution.py:488
  55.5 1.3 %collective-permute-start.8 = (bf16[3,72,128]{2,1,0:T(8,128)(2,1)S(1)}, bf16[3,72,128]{2,1,0:T(8,128)(2,1)S(1)}, u32[]{:S(2)}, u32[]{:S(2)}) collective-permute-start(bf16[3,72,128]{2,1,0:T(8,128)(2,1)S(1)} %get-tuple-element.51), channel_id=1, source_target_pairs={{0,1},{1,2},{2,3},{3,4},{4,5},{5,6},{6,7},{7,8},{8,9},{9,10},{10,1... | collective-permute-start | bytes 165896 | tf_op jit(solution)/shard_map/ppermute | solution.py:471
  55.6 3.6 %collective-permute-start.9 = (bf16[3,72,128]{2,1,0:T(8,128)(2,1)S(1)}, bf16[3,72,128]{2,1,0:T(8,128)(2,1)S(1)}, u32[]{:S(2)}, u32[]{:S(2)}) collective-permute-start(bf16[3,72,128]{2,1,0:T(8,128)(2,1)S(1)} %get-tuple-element.52), channel_id=1, source_target_pairs={{0,15},{1,0},{2,1},{3,2},{4,3},{5,4},{6,5},{7,6},{8,7},{9,8},{10,9... | collective-permute-start | bytes 165896 | tf_op jit(solution)/shard_map/ppermute | solution.py:471
  59.2 4.1 %collective-permute-start.11 = (bf16[3,72,128]{2,1,0:T(8,128)(2,1)S(1)}, bf16[3,72,128]{2,1,0:T(8,128)(2,1)S(1)}, u32[]{:S(2)}, u32[]{:S(2)}) collective-permute-start(bf16[3,72,128]{2,1,0:T(8,128)(2,1)S(1)} %pad_maximum_fusion), channel_id=1, source_target_pairs={{0,13},{1,14},{2,15},{3,0},{4,1},{5,2},{6,3},{7,4},{8,5},{9,6},{10... | collective-permute-start | bytes 165896 | tf_op jit(solution)/shard_map/ppermute | solution.py:471
  60.1 7.3 %collective-permute-start.10 = (bf16[3,72,128]{2,1,0:T(8,128)(2,1)S(1)}, bf16[3,72,128]{2,1,0:T(8,128)(2,1)S(1)}, u32[]{:S(2)}, u32[]{:S(2)}) collective-permute-start(bf16[3,72,128]{2,1,0:T(8,128)(2,1)S(1)} %pad_maximum_fusion), channel_id=1, source_target_pairs={{0,3},{1,4},{2,5},{3,6},{4,7},{5,8},{6,9},{7,10},{8,11},{9,12},{10... | collective-permute-start | bytes 165896 | tf_op jit(solution)/shard_map/ppermute | solution.py:471
where the time goes:
time: 72.7 us; the launch traced here: 72.3 us
  waiting for transfers between devices  35.5 us (49%)
  starting transfers between devices  19.5 us (27%)
  Pallas kernels  15.7 us (22%)
  between operations  0.93 us (1%)
    ppermute x8, waiting for transfers between devices, per_device(): nexts[across] = lax.ppermute(nexts[across], 'tile', pairs)  28.2 us
    ppermute x8, starting transfers between devices, per_device(): nexts[across] = lax.ppermute(nexts[across], 'tile', pairs)  10.3 us
    ppermute x4, waiting for transfers between devices, from_shift(): lax.ppermute(value, 'tile', [(i, (i - shift) % count) for i in range(coun...  7.26 us
    all_to_all x1, starting transfers between devices, per_device(): lax.all_to_all(same, 'tile', 0, 0, axis_index_groups=[[c * column_rows +...  6.52 us
    pallas_call x1, Pallas kernels, regrid(): pl.pallas_call(functools.partial(regrid_kernel, column_rows), in_specs=[s...  6.15 us
    pallas_call x1, Pallas kernels, convolutions(): pl.pallas_call(functools.partial(conv_kernel, column_rows), in_specs=[vme...  4.84 us
    pallas_call x1, Pallas kernels, gather_rows(): pl.pallas_call(functools.partial(gather_kernel, column_rows), in_specs=[s...  2.76 us
    ppermute x4, starting transfers between devices, from_shift(): lax.ppermute(value, 'tile', [(i, (i - shift) % count) for i in range(coun...  2.67 us
  transfers between devices with their start and end apart: 13, of which 8 were waited for; matrix products, arithmetic and copies ran while one was open for 1% of the time, Pallas kernels for 3%

commit v1 on v0

--- a/solution.py
+++ b/solution.py
@@ -479,13 +479,17 @@
     field = source.reshape(ROWS, CHANNELS, BLOCK).transpose(1, 0, 2).reshape(-1, BLOCK)
     same, *nexts = regrid(block_target, block_source, field, weights, column_rows)
 
-    for across in (0, 7, 3, 6, 2, 5, 1, 4):
+    def to_next(across):
         pairs = [
             (c * column_rows + p, (c ^ across) * column_rows + p + 1)
             for c in range(TILE_COLS)
             for p in range(column_rows - 1)
         ]
-        nexts[across] = lax.ppermute(nexts[across], "tile", pairs)
+        return lax.ppermute(nexts[across], "tile", pairs)
+
+    early = [to_next(across) for across in (7, 0, 1)]
+    same, *early = lax.optimization_barrier((same, *early))
+    late = [to_next(across) for across in (6, 5, 4, 3, 2)]
     same = lax.all_to_all(
         same,
         "tile",
@@ -496,6 +500,7 @@
         ],
         tiled=True,
     )
+    nexts = early + late
 
     gain = jnp.broadcast_to(
         jnp.pad(norm_gain, (0, PADDED - CHANNELS))[:, None], (PADDED, BLOCK)

time: 72.7 us -> 83.1 us (1.14); the launches traced: 72.3 us -> 81.7 us
  waiting for transfers between devices: 35.5 us -> 47.3 us
  starting transfers between devices: 19.5 us -> 17.1 us
    ppermute x8, waiting for transfers between devices: 28.2 us -> 40.3 us  [to_next(): return lax.ppermute(nexts[across], 'tile', pairs)]
    all_to_all x1, starting transfers between devices: 6.52 us -> 4.25 us  [per_device(): lax.all_to_all(same, 'tile', 0, 0, axis_index_groups=[[c * column_rows +...]
  transfers between devices with their start and end apart: 13 -> 13, of which waited for: 8 -> 9; matrix products, arithmetic and copies ran while one was open for 1% -> 1% of each run, Pallas kernels for 3% -> 2%
where the time goes in v1:
time: 83.1 us; the launch traced here: 81.7 us
  waiting for transfers between devices  47.3 us (57%)
  starting transfers between devices  17.1 us (21%)
  Pallas kernels  15.7 us (19%)
  between operations  0.86 us (1%)
    ppermute x8, waiting for transfers between devices, to_next(): return lax.ppermute(nexts[across], 'tile', pairs)  40.3 us
    ppermute x8, starting transfers between devices, to_next(): return lax.ppermute(nexts[across], 'tile', pairs)  10.5 us
    ppermute x4, waiting for transfers between devices, from_shift(): lax.ppermute(value, 'tile', [(i, (i - shift) % count) for i in range(coun...  7 us
    pallas_call x1, Pallas kernels, regrid(): pl.pallas_call(functools.partial(regrid_kernel, column_rows), in_specs=[s...  6.15 us
    pallas_call x1, Pallas kernels, convolutions(): pl.pallas_call(functools.partial(conv_kernel, column_rows), in_specs=[vme...  4.82 us
    all_to_all x1, starting transfers between devices, per_device(): lax.all_to_all(same, 'tile', 0, 0, axis_index_groups=[[c * column_rows +...  4.25 us
    pallas_call x1, Pallas kernels, gather_rows(): pl.pallas_call(functools.partial(gather_kernel, column_rows), in_specs=[s...  2.76 us
    ppermute x4, starting transfers between devices, from_shift(): lax.ppermute(value, 'tile', [(i, (i - shift) % count) for i in range(coun...  2.35 us
  transfers between devices with their start and end apart: 13, of which 9 were waited for; matrix products, arithmetic and copies ran while one was open for 1% of the time, Pallas kernels for 2%

profile of v1, /device:TPU:1, one launch (start us, length us, event | category | flops | bytes accessed | tf_op | source)
XLA Modules:
  0.0 81.7 jit_solution(11631984993005411053)
XLA Ops:
  0.6 6.2 %regrid.1 = (bf16[64,72,128]{2,1,0:T(8,128)(2,1)}, bf16[8,72,128]{2,1,0:T(8,128)(2,1)}, bf16[8,72,128]{2,1,0:T(8,128)(2,1)}, bf16[8,72,128]{2,1,0:T(8,128)(2,1)}...) custom-call(s32[96]{0:T(128)} %target_ref.1, ...), custom_call_target="tpu_custom_call" | custom-call | tf_op jit(solution)/shard_map/regrid/pallas_call | solution.py:146
  6.8 1.3 %collective-permute-start = (bf16[8,72,128]{2,1,0:T(8,128)(2,1)}, bf16[8,72,128]{2,1,0:T(8,128)(2,1)S(1)}, u32[]{:S(2)}, u32[]{:S(2)}) collective-permute-start(bf16[8,72,128]{2,1,0:T(8,128)(2,1)} %get-tuple-element.33), channel_id=1, source_target_pairs={{0,15},{2,13},{4,11},{6,9},{8,7},{10,5},{12,3},{14,1},{16,31},{18,... | collective-permute-start | bytes 442376 | tf_op jit(solution)/shard_map/ppermute | solution.py:488
  8.1 1.3 %collective-permute-start.1 = (bf16[8,72,128]{2,1,0:T(8,128)(2,1)}, bf16[8,72,128]{2,1,0:T(8,128)(2,1)S(1)}, u32[]{:S(2)}, u32[]{:S(2)}) collective-permute-start(bf16[8,72,128]{2,1,0:T(8,128)(2,1)} %get-tuple-element.34), channel_id=1, source_target_pairs={{0,1},{2,3},{4,5},{6,7},{8,9},{10,11},{12,13},{14,15},{16,17},{18,... | collective-permute-start | bytes 442376 | tf_op jit(solution)/shard_map/ppermute | solution.py:488
  9.4 1.3 %collective-permute-start.2 = (bf16[8,72,128]{2,1,0:T(8,128)(2,1)}, bf16[8,72,128]{2,1,0:T(8,128)(2,1)S(1)}, u32[]{:S(2)}, u32[]{:S(2)}) collective-permute-start(bf16[8,72,128]{2,1,0:T(8,128)(2,1)} %get-tuple-element.35), channel_id=1, source_target_pairs={{0,3},{2,1},{4,7},{6,5},{8,11},{10,9},{12,15},{14,13},{16,19},{18,... | collective-permute-start | bytes 442376 | tf_op jit(solution)/shard_map/ppermute | solution.py:488
  10.7 6.2 %collective-permute-done.rest_0_ = bf16[8,72,128]{2,1,0:T(8,128)(2,1)S(1)} collective-permute-done((bf16[8,72,128]{2,1,0:T(8,128)(2,1)}, bf16[8,72,128]{2,1,0:T(8,128)(2,1)S(1)}, u32[]{:S(2)}, u32[]{:S(2)}) %collective-permute-start) | collective-permute-done | bytes 147488 | tf_op jit(solution)/shard_map/ppermute | solution.py:488
  16.9 0.0 collective-permute-done.1.rest_1_
  16.9 3.0 %collective-permute-done.2.rest_2_ = bf16[8,72,128]{2,1,0:T(8,128)(2,1)S(1)} collective-permute-done((bf16[8,72,128]{2,1,0:T(8,128)(2,1)}, bf16[8,72,128]{2,1,0:T(8,128)(2,1)S(1)}, u32[]{:S(2)}, u32[]{:S(2)}) %collective-permute-start.2) | collective-permute-done | bytes 147488 | tf_op jit(solution)/shard_map/ppermute | solution.py:488
  19.9 0.0 copy-start.5
  19.9 0.0 copy-start.4
  19.9 0.0 copy-start.3
  19.9 0.0 copy-start.1
  19.9 0.0 copy-start.2
  20.0 4.3 %all-to-all-start = ((bf16[64,72,128]{2,1,0:T(8,128)(2,1)}), bf16[64,72,128]{2,1,0:T(8,128)(2,1)S(1)}, u32[]{:S(2)}, u32[]{:S(2)}) async-start(bf16[64,72,128]{2,1,0:T(8,128)(2,1)} %get-tuple-element.36), calls=%async_computation | async-start | bytes 2359296 | tf_op jit(solution)/shard_map/all_to_all | solution.py:493
  24.2 0.0 copy-start
  24.2 1.4 %collective-permute-start.3 = (bf16[8,72,128]{2,1,0:T(8,128)(2,1)}, bf16[8,72,128]{2,1,0:T(8,128)(2,1)S(1)}, u32[]{:S(2)}, u32[]{:S(2)}) collective-permute-start(bf16[8,72,128]{2,1,0:T(8,128)(2,1)} %get-tuple-element.40), channel_id=1, source_target_pairs={{0,13},{2,15},{4,9},{6,11},{8,5},{10,7},{12,1},{14,3},{16,29},{18,... | collective-permute-start | bytes 442376 | tf_op jit(solution)/shard_map/ppermute | solution.py:488
  25.7 1.3 %collective-permute-start.4 = (bf16[8,72,128]{2,1,0:T(8,128)(2,1)}, bf16[8,72,128]{2,1,0:T(8,128)(2,1)S(1)}, u32[]{:S(2)}, u32[]{:S(2)}) collective-permute-start(bf16[8,72,128]{2,1,0:T(8,128)(2,1)} %get-tuple-element.41), channel_id=1, source_target_pairs={{0,11},{2,9},{4,15},{6,13},{8,3},{10,1},{12,7},{14,5},{16,27},{18,... | collective-permute-start | bytes 442376 | tf_op jit(solution)/shard_map/ppermute | solution.py:488
  27.0 0.0 copy-done.5
  27.0 1.3 %collective-permute-start.5 = (bf16[8,72,128]{2,1,0:T(8,128)(2,1)S(1)}, bf16[8,72,128]{2,1,0:T(8,128)(2,1)S(1)}, u32[]{:S(2)}, u32[]{:S(2)}) collective-permute-start(bf16[8,72,128]{2,1,0:T(8,128)(2,1)S(1)} %copy-done.5), channel_id=1, source_target_pairs={{0,9},{2,11},{4,13},{6,15},{8,1},{10,3},{12,5},{14,7},{16,25},{18,... | collective-permute-start | bytes 442376 | tf_op jit(solution)/shard_map/ppermute | solution.py:488
  28.3 0.0 copy-done.4
  28.3 1.3 %collective-permute-start.6 = (bf16[8,72,128]{2,1,0:T(8,128)(2,1)S(1)}, bf16[8,72,128]{2,1,0:T(8,128)(2,1)S(1)}, u32[]{:S(2)}, u32[]{:S(2)}) collective-permute-start(bf16[8,72,128]{2,1,0:T(8,128)(2,1)S(1)} %copy-done.4), channel_id=1, source_target_pairs={{0,7},{2,5},{4,3},{6,1},{8,15},{10,13},{12,11},{14,9},{16,23},{18,... | collective-permute-start | bytes 442376 | tf_op jit(solution)/shard_map/ppermute | solution.py:488
  29.6 0.0 copy-done.3
  29.6 1.3 %collective-permute-start.7 = (bf16[8,72,128]{2,1,0:T(8,128)(2,1)S(1)}, bf16[8,72,128]{2,1,0:T(8,128)(2,1)S(1)}, u32[]{:S(2)}, u32[]{:S(2)}) collective-permute-start(bf16[8,72,128]{2,1,0:T(8,128)(2,1)S(1)} %copy-done.3), channel_id=1, source_target_pairs={{0,5},{2,7},{4,1},{6,3},{8,13},{10,15},{12,9},{14,11},{16,21},{18,... | collective-permute-start | bytes 442376 | tf_op jit(solution)/shard_map/ppermute | solution.py:488
  30.9 0.0 copy-done.1
  30.9 0.1 copy.17
  31.0 0.1 reshape.32.first_taps_ref
  31.2 0.0 copy-done.2
  31.3 0.1 copy.16
  31.3 0.1 reshape.34.second_taps_ref
  31.5 0.0 copy-done.6
  31.5 17.9 %collective-permute-done.3.rest_3_ = bf16[8,72,128]{2,1,0:T(8,128)(2,1)S(1)} collective-permute-done((bf16[8,72,128]{2,1,0:T(8,128)(2,1)}, bf16[8,72,128]{2,1,0:T(8,128)(2,1)S(1)}, u32[]{:S(2)}, u32[]{:S(2)}) %collective-permute-start.3) | collective-permute-done | bytes 147488 | tf_op jit(solution)/shard_map/ppermute | solution.py:488
  49.4 12.7 %collective-permute-done.4.rest_4_ = bf16[8,72,128]{2,1,0:T(8,128)(2,1)S(1)} collective-permute-done((bf16[8,72,128]{2,1,0:T(8,128)(2,1)}, bf16[8,72,128]{2,1,0:T(8,128)(2,1)S(1)}, u32[]{:S(2)}, u32[]{:S(2)}) %collective-permute-start.4) | collective-permute-done | bytes 147488 | tf_op jit(solution)/shard_map/ppermute | solution.py:488
  62.1 0.5 collective-permute-done.5.rest_5_
  62.6 0.0 collective-permute-done.6.rest_6_
  62.6 0.0 collective-permute-done.7.rest_7_
  62.6 0.0 all-to-all-done.same
  62.6 0.1 broadcast_in_dim.12.gain_ref
  62.7 0.0 copy-done
  62.7 2.8 %gather_rows.1 = (bf16[32,72,128]{2,1,0:T(8,128)(2,1)S(1)}, bf16[32,72,128]{2,1,0:T(8,128)(2,1)S(1)}, bf16[3,72,128]{2,1,0:T(8,128)(2,1)S(1)}, bf16[3,72,128]{2,1,0:T(8,128)(2,1)S(1)}, bf16[72,128]{1,0:T(8,128)(2,1)S(1)}) custom-call(s32[1,2]{1,0:T(1,128)S(1)} %copy-done, f32[72,128]{1,0:T(8,128)S(1)} %broadcast_in_dim.12.gain_ref, ...), custom_call_target="tpu_custom_call" | custom-call | tf_op jit(solution)/shard_map/gather_rows/pallas_call | solution.py:249
  65.5 0.1 collective-permute-start.8
  65.5 0.5 collective-permute-start.9
  66.0 0.7 collective-permute-done.8.above
  66.8 2.7 %collective-permute-done.9.below = bf16[3,72,128]{2,1,0:T(8,128)(2,1)S(1)} collective-permute-done((bf16[3,72,128]{2,1,0:T(8,128)(2,1)S(1)}, bf16[3,72,128]{2,1,0:T(8,128)(2,1)S(1)}, u32[]{:S(2)}, u32[]{:S(2)}) %collective-permute-start.9) | collective-permute-done | bytes 55328 | tf_op jit(solution)/shard_map/ppermute | solution.py:471
  69.5 1.1 %collective-permute-start.11 = (bf16[3,72,128]{2,1,0:T(8,128)(2,1)S(1)}, bf16[3,72,128]{2,1,0:T(8,128)(2,1)S(1)}, u32[]{:S(2)}, u32[]{:S(2)}) collective-permute-start(bf16[3,72,128]{2,1,0:T(8,128)(2,1)S(1)} %pad_maximum_fusion), channel_id=1, source_target_pairs={{0,13},{1,14},{2,15},{3,0},{4,1},{5,2},{6,3},{7,4},{8,5},{9,6},{10... | collective-permute-start | bytes 165896 | tf_op jit(solution)/shard_map/ppermute | solution.py:471
  70.6 0.7 collective-permute-start.10
  71.3 2.0 %channels_first.1 = bf16[2208,128]{1,0:T(8,128)(2,1)} custom-call(bf16[32,72,128]{2,1,0:T(8,128)(2,1)S(1)} %get-tuple-element.55.field.gridded), custom_call_target="tpu_custom_call" | custom-call | tf_op jit(solution)/shard_map/channels_first/pallas_call | solution.py:272
  73.3 0.1 collective-permute-done.11.rest_1_
  73.4 3.4 %collective-permute-done.10.rest_0_ = bf16[3,72,128]{2,1,0:T(8,128)(2,1)S(1)} collective-permute-done((bf16[3,72,128]{2,1,0:T(8,128)(2,1)S(1)}, bf16[3,72,128]{2,1,0:T(8,128)(2,1)S(1)}, u32[]{:S(2)}, u32[]{:S(2)}) %collective-permute-start.10) | collective-permute-done | bytes 55328 | tf_op jit(solution)/shard_map/ppermute | solution.py:471
  76.8 4.8 %convolutions.1 = bf16[2208,128]{1,0:T(8,128)(2,1)} custom-call(bf16[216,216]{1,0:T(8,128)(2,1)S(1)} %reshape.32.first_taps_ref, bf16[216,216]{1,0:T(8,128)(2,1)S(1)} %reshape.34.second_taps_ref, bf16[32,72,128]{2,1,0:T(8,128)(2,1)S(1)} %get-tuple-element.58.field, bf16[32,72,128]{2,1,0:T(8,128)(2,1)S(1)} %get-tuple-element.55.field.gridded, ...), custom_call_target="tpu_custom_call" | custom-call | tf_op jit(solution)/shard_map/convolutions/pallas_call | solution.py:448
  (7 shorter events, 0.1 us)
Async XLA Ops:
  6.8 10.1 %collective-permute-start = (bf16[8,72,128]{2,1,0:T(8,128)(2,1)}, bf16[8,72,128]{2,1,0:T(8,128)(2,1)S(1)}, u32[]{:S(2)}, u32[]{:S(2)}) collective-permute-start(bf16[8,72,128]{2,1,0:T(8,128)(2,1)} %get-tuple-element.33), channel_id=1, source_target_pairs={{0,15},{2,13},{4,11},{6,9},{8,7},{10,5},{12,3},{14,1},{16,31},{18,... | collective-permute-start | bytes 442376 | tf_op jit(solution)/shard_map/ppermute | solution.py:488
  8.1 8.8 %collective-permute-start.1 = (bf16[8,72,128]{2,1,0:T(8,128)(2,1)}, bf16[8,72,128]{2,1,0:T(8,128)(2,1)S(1)}, u32[]{:S(2)}, u32[]{:S(2)}) collective-permute-start(bf16[8,72,128]{2,1,0:T(8,128)(2,1)} %get-tuple-element.34), channel_id=1, source_target_pairs={{0,1},{2,3},{4,5},{6,7},{8,9},{10,11},{12,13},{14,15},{16,17},{18,... | collective-permute-start | bytes 442376 | tf_op jit(solution)/shard_map/ppermute | solution.py:488
  9.4 10.5 %collective-permute-start.2 = (bf16[8,72,128]{2,1,0:T(8,128)(2,1)}, bf16[8,72,128]{2,1,0:T(8,128)(2,1)S(1)}, u32[]{:S(2)}, u32[]{:S(2)}) collective-permute-start(bf16[8,72,128]{2,1,0:T(8,128)(2,1)} %get-tuple-element.35), channel_id=1, source_target_pairs={{0,3},{2,1},{4,7},{6,5},{8,11},{10,9},{12,15},{14,13},{16,19},{18,... | collective-permute-start | bytes 442376 | tf_op jit(solution)/shard_map/ppermute | solution.py:488
  19.9 7.0 %copy-start.5 = (bf16[8,72,128]{2,1,0:T(8,128)(2,1)S(1)}, bf16[8,72,128]{2,1,0:T(8,128)(2,1)}, u32[]{:S(2)}) copy-start(bf16[8,72,128]{2,1,0:T(8,128)(2,1)} %get-tuple-element.42) | copy-start | bytes 442372
  19.9 8.3 %copy-start.4 = (bf16[8,72,128]{2,1,0:T(8,128)(2,1)S(1)}, bf16[8,72,128]{2,1,0:T(8,128)(2,1)}, u32[]{:S(2)}) copy-start(bf16[8,72,128]{2,1,0:T(8,128)(2,1)} %get-tuple-element.43) | copy-start | bytes 442372
  19.9 9.6 %copy-start.3 = (bf16[8,72,128]{2,1,0:T(8,128)(2,1)S(1)}, bf16[8,72,128]{2,1,0:T(8,128)(2,1)}, u32[]{:S(2)}) copy-start(bf16[8,72,128]{2,1,0:T(8,128)(2,1)} %get-tuple-element.44) | copy-start | bytes 442372
  19.9 11.0 %copy-start.1 = (bf16[9,69,69]{2,1,0:T(8,128)(2,1)S(1)}, bf16[9,69,69]{2,1,0:T(8,128)(2,1)}, u32[]{:S(2)}) copy-start(bf16[9,69,69]{2,1,0:T(8,128)(2,1)} %param.14) | copy-start | bytes 257098
  19.9 11.2 %copy-start.2 = (bf16[9,69,69]{2,1,0:T(8,128)(2,1)S(1)}, bf16[9,69,69]{2,1,0:T(8,128)(2,1)}, u32[]{:S(2)}) copy-start(bf16[9,69,69]{2,1,0:T(8,128)(2,1)} %param.15) | copy-start | bytes 257098
  20.0 42.7 %all-to-all-start = ((bf16[64,72,128]{2,1,0:T(8,128)(2,1)}), bf16[64,72,128]{2,1,0:T(8,128)(2,1)S(1)}, u32[]{:S(2)}, u32[]{:S(2)}) async-start(bf16[64,72,128]{2,1,0:T(8,128)(2,1)} %get-tuple-element.36), calls=%async_computation | async-start | bytes 2359296 | tf_op jit(solution)/shard_map/all_to_all | solution.py:493
  24.2 7.3 %copy-start.6 = (f32[69]{0:T(128)S(1)}, f32[69]{0:T(128)}, u32[]{:S(2)}) copy-start(f32[69]{0:T(128)} %param.13) | copy-start | bytes 832
  24.2 38.5 %copy-start = (s32[1,2]{1,0:T(1,128)S(1)}, s32[1,2]{1,0:T(1,128)}, u32[]{:S(2)}) copy-start(s32[1,2]{1,0:T(1,128)} %flip_ref.1) | copy-start | bytes 28
  24.2 25.2 %collective-permute-start.3 = (bf16[8,72,128]{2,1,0:T(8,128)(2,1)}, bf16[8,72,128]{2,1,0:T(8,128)(2,1)S(1)}, u32[]{:S(2)}, u32[]{:S(2)}) collective-permute-start(bf16[8,72,128]{2,1,0:T(8,128)(2,1)} %get-tuple-element.40), channel_id=1, source_target_pairs={{0,13},{2,15},{4,9},{6,11},{8,5},{10,7},{12,1},{14,3},{16,29},{18,... | collective-permute-start | bytes 442376 | tf_op jit(solution)/shard_map/ppermute | solution.py:488
  25.7 36.5 %collective-permute-start.4 = (bf16[8,72,128]{2,1,0:T(8,128)(2,1)}, bf16[8,72,128]{2,1,0:T(8,128)(2,1)S(1)}, u32[]{:S(2)}, u32[]{:S(2)}) collective-permute-start(bf16[8,72,128]{2,1,0:T(8,128)(2,1)} %get-tuple-element.41), channel_id=1, source_target_pairs={{0,11},{2,9},{4,15},{6,13},{8,3},{10,1},{12,7},{14,5},{16,27},{18,... | collective-permute-start | bytes 442376 | tf_op jit(solution)/shard_map/ppermute | solution.py:488
  27.0 35.6 %collective-permute-start.5 = (bf16[8,72,128]{2,1,0:T(8,128)(2,1)S(1)}, bf16[8,72,128]{2,1,0:T(8,128)(2,1)S(1)}, u32[]{:S(2)}, u32[]{:S(2)}) collective-permute-start(bf16[8,72,128]{2,1,0:T(8,128)(2,1)S(1)} %copy-done.5), channel_id=1, source_target_pairs={{0,9},{2,11},{4,13},{6,15},{8,1},{10,3},{12,5},{14,7},{16,25},{18,... | collective-permute-start | bytes 442376 | tf_op jit(solution)/shard_map/ppermute | solution.py:488
  28.3 34.3 %collective-permute-start.6 = (bf16[8,72,128]{2,1,0:T(8,128)(2,1)S(1)}, bf16[8,72,128]{2,1,0:T(8,128)(2,1)S(1)}, u32[]{:S(2)}, u32[]{:S(2)}) collective-permute-start(bf16[8,72,128]{2,1,0:T(8,128)(2,1)S(1)} %copy-done.4), channel_id=1, source_target_pairs={{0,7},{2,5},{4,3},{6,1},{8,15},{10,13},{12,11},{14,9},{16,23},{18,... | collective-permute-start | bytes 442376 | tf_op jit(solution)/shard_map/ppermute | solution.py:488
  29.6 33.0 %collective-permute-start.7 = (bf16[8,72,128]{2,1,0:T(8,128)(2,1)S(1)}, bf16[8,72,128]{2,1,0:T(8,128)(2,1)S(1)}, u32[]{:S(2)}, u32[]{:S(2)}) collective-permute-start(bf16[8,72,128]{2,1,0:T(8,128)(2,1)S(1)} %copy-done.3), channel_id=1, source_target_pairs={{0,5},{2,7},{4,1},{6,3},{8,13},{10,15},{12,9},{14,11},{16,21},{18,... | collective-permute-start | bytes 442376 | tf_op jit(solution)/shard_map/ppermute | solution.py:488
  65.5 1.3 %collective-permute-start.8 = (bf16[3,72,128]{2,1,0:T(8,128)(2,1)S(1)}, bf16[3,72,128]{2,1,0:T(8,128)(2,1)S(1)}, u32[]{:S(2)}, u32[]{:S(2)}) collective-permute-start(bf16[3,72,128]{2,1,0:T(8,128)(2,1)S(1)} %get-tuple-element.59), channel_id=1, source_target_pairs={{0,1},{1,2},{2,3},{3,4},{4,5},{5,6},{6,7},{7,8},{8,9},{9,10},{10,1... | collective-permute-start | bytes 165896 | tf_op jit(solution)/shard_map/ppermute | solution.py:471
  65.5 3.9 %collective-permute-start.9 = (bf16[3,72,128]{2,1,0:T(8,128)(2,1)S(1)}, bf16[3,72,128]{2,1,0:T(8,128)(2,1)S(1)}, u32[]{:S(2)}, u32[]{:S(2)}) collective-permute-start(bf16[3,72,128]{2,1,0:T(8,128)(2,1)S(1)} %get-tuple-element.60), channel_id=1, source_target_pairs={{0,15},{1,0},{2,1},{3,2},{4,3},{5,4},{6,5},{7,6},{8,7},{9,8},{10,9... | collective-permute-start | bytes 165896 | tf_op jit(solution)/shard_map/ppermute | solution.py:471
  69.5 3.9 %collective-permute-start.11 = (bf16[3,72,128]{2,1,0:T(8,128)(2,1)S(1)}, bf16[3,72,128]{2,1,0:T(8,128)(2,1)S(1)}, u32[]{:S(2)}, u32[]{:S(2)}) collective-permute-start(bf16[3,72,128]{2,1,0:T(8,128)(2,1)S(1)} %pad_maximum_fusion), channel_id=1, source_target_pairs={{0,13},{1,14},{2,15},{3,0},{4,1},{5,2},{6,3},{7,4},{8,5},{9,6},{10... | collective-permute-start | bytes 165896 | tf_op jit(solution)/shard_map/ppermute | solution.py:471
  70.6 6.3 %collective-permute-start.10 = (bf16[3,72,128]{2,1,0:T(8,128)(2,1)S(1)}, bf16[3,72,128]{2,1,0:T(8,128)(2,1)S(1)}, u32[]{:S(2)}, u32[]{:S(2)}) collective-permute-start(bf16[3,72,128]{2,1,0:T(8,128)(2,1)S(1)} %pad_maximum_fusion), channel_id=1, source_target_pairs={{0,3},{1,4},{2,5},{3,6},{4,7},{5,8},{6,9},{7,10},{8,11},{9,12},{10... | collective-permute-start | bytes 165896 | tf_op jit(solution)/shard_map/ppermute | solution.py:471
